TPU v7x, 128 devices: a whole 4x4x4 slice. The times are simulated.
128 devices in a mesh: seq: 32 (over z_hi, x, y), fsdp: 4 (over z_lo, core).
Axes of the slice: x: 4, y: 4, z: 4 (z_hi: 2, z_lo: 2; z = z_hi * 2 + z_lo), core: 2. Of those that a mesh axis runs over, the one named last changes fastest.
Arguments:
- hidden_in: bfloat16 [4, 16384, 640], P('fsdp', 'seq'), may hold values from -6 to 6
- cotangent: bfloat16 [4, 16384, 640], P('fsdp', 'seq'), may hold values from -6 to 6
- positions: int32 [4, 16384], P('fsdp', 'seq'), may hold values from 0 to 15871, as said below
- query_weight: bfloat16 [640, 1024], P('fsdp'), may hold values from -0.25 to 0.25
- key_weight: bfloat16 [640, 256], P('fsdp'), may hold values from -0.25 to 0.25
- value_weight: bfloat16 [640, 256], P('fsdp'), may hold values from -0.25 to 0.25
- output_weight: bfloat16 [1024, 640], P('fsdp'), may hold values from -0.1875 to 0.1875
- gate_weight: bfloat16 [640, 2048], P('fsdp'), may hold values from -0.25 to 0.25
- up_weight: bfloat16 [640, 2048], P('fsdp'), may hold values from -0.25 to 0.25
- down_weight: bfloat16 [2048, 640], P('fsdp'), may hold values from -0.125 to 0.125
- norm_in: bfloat16 [640], P('fsdp'), may hold values from 0.5 to 1.5
- norm_attn: bfloat16 [640], P('fsdp'), may hold values from 0.5 to 1.5
- norm_ffn_in: bfloat16 [640], P('fsdp'), may hold values from 0.5 to 1.5
- norm_ffn_out: bfloat16 [640], P('fsdp'), may hold values from 0.5 to 1.5
- norm_query: bfloat16 [256], P('fsdp'), may hold values from 0.25 to 1.75
- norm_key: bfloat16 [256], P('fsdp'), may hold values from 0.25 to 1.75
Outputs:
- layer_out: bfloat16 [4, 16384, 640], P('fsdp', 'seq')
- grad_in: bfloat16 [4, 16384, 640], P('fsdp', 'seq')
- grad_query: float32 [640, 1024], P('fsdp')
- grad_key: float32 [640, 256], P('fsdp')
- grad_value: float32 [640, 256], P('fsdp')
- grad_output: float32 [1024, 640], P('fsdp')
- grad_gate: float32 [640, 2048], P('fsdp')
- grad_up: float32 [640, 2048], P('fsdp')
- grad_down: float32 [2048, 640], P('fsdp')
- grad_norm_in: float32 [640], P('fsdp')
- grad_norm_attn: float32 [640], P('fsdp')
- grad_norm_ffn_in: float32 [640], P('fsdp')
- grad_norm_ffn_out: float32 [640], P('fsdp')
- grad_norm_query: float32 [256], P('fsdp')
- grad_norm_key: float32 [256], P('fsdp')
Inputs may be any that keep to these rules, and one draw needn't show every extreme that they name: `positions`: within each sequence the offsets rise by one from token to token and restart at 0 where a document begins (token 0 begins one); one document begins within the first 512 tokens and spans exactly 15872 tokens.
All inputs are finite; a program needn't handle non-finite values.
Results may differ from a plain program's by a relative error of at most 0.03.
Values may be sent and summed in bfloat16 or wider, within the bound.
No kernel may reach another device: no remote copies, remote signals or barrier semaphores. Data moves between devices by JAX's collectives and lax.ppermute only.
A program may use at most 128 MiB of HBM per device.

v0:
```python
import jax
import jax.numpy as jnp
from jax import lax
from jax.sharding import PartitionSpec as P

WINDOW = 512


epsilon = 1e-06
rope_base = 10000.0
masked_value = -1e30


def in_one_piece(arrays, axis, dim, along):
    widths = [a.shape[along] for a in arrays]
    both = jnp.concatenate(arrays, axis=along)
    whole = lax.all_gather(both, axis, axis=dim, tiled=True)
    return tuple(jnp.split(whole, [sum(widths[:k]) for k in range(1, len(widths))], axis=along))


def shifted(value, axis, steps):
    count = lax.axis_size(axis)
    first, last = (max(0, -steps), min(count, count - steps))
    return lax.ppermute(value, axis, [(source, source + steps) for source in range(first, last)])


def sent_together(arrays, axis, dim, along):
    widths = [a.shape[along] for a in arrays]
    both = jnp.concatenate(arrays, axis=along)
    whole = lax.psum_scatter(both, axis, scatter_dimension=dim, tiled=True)
    return tuple(jnp.split(whole, [sum(widths[:k]) for k in range(1, len(widths))], axis=along))


def norm_rows(values, gain):
    return values * lax.rsqrt(jnp.mean(values * values, axis=-1, keepdims=True) + epsilon) * gain


def turn_pairs(values, cosine, sine_part):
    half_width = values.shape[-1] // 2
    leading = values[..., :half_width]
    trailing = values[..., half_width:]
    return jnp.concatenate(
        [leading * cosine - trailing * sine_part, trailing * cosine + leading * sine_part], axis=-1
    )


def body(
    hidden_in,
    cotangent,
    positions,
    query_weight,
    key_weight,
    value_weight,
    output_weight,
    gate_weight,
    up_weight,
    down_weight,
    norm_in,
    norm_attn,
    norm_ffn_in,
    norm_ffn_out,
    norm_query,
    norm_key,
):
    gathered = (
        *in_one_piece((query_weight, key_weight, value_weight), "fsdp", 0, 1),
        lax.all_gather(output_weight, "fsdp", axis=0, tiled=True),
        *in_one_piece((gate_weight, up_weight), "fsdp", 0, 1),
        lax.all_gather(down_weight, "fsdp", axis=0, tiled=True),
        lax.all_gather(norm_in, "fsdp", axis=0, tiled=True),
        lax.all_gather(norm_attn, "fsdp", axis=0, tiled=True),
        lax.all_gather(norm_ffn_in, "fsdp", axis=0, tiled=True),
        lax.all_gather(norm_ffn_out, "fsdp", axis=0, tiled=True),
        lax.all_gather(norm_query, "fsdp", axis=0, tiled=True),
        lax.all_gather(norm_key, "fsdp", axis=0, tiled=True),
    )
    query_full, key_full, value_full, output_full, gate_full, upward_full, down_full = gathered[:7]
    gain_in, gain_attn, gain_ffn_in, gain_ffn_out, gain_query, gain_key = [
        gain.astype(jnp.float32) for gain in gathered[7:]
    ]
    inputs = hidden_in[0].astype(jnp.float32)
    offsets = positions[0]
    tokens = inputs.shape[0]
    head_width = gain_query.shape[0]
    heads = query_full.shape[1] // head_width
    half_width = head_width // 2
    scale = head_width ** (-0.5)
    powers = jnp.arange(half_width, dtype=jnp.float32) * (2.0 / head_width)
    angles = offsets.astype(jnp.float32)[:, None] * (rope_base ** (-powers))[None, :]
    cosine = jnp.cos(angles)[:, None, :]
    sine_part = jnp.sin(angles)[:, None, :]
    normed_f, pull_in = jax.vjp(norm_rows, inputs, gain_in)
    normed = normed_f.astype(jnp.bfloat16)
    query_proj = jnp.dot(normed, query_full, preferred_element_type=jnp.float32)
    key_proj = jnp.dot(normed, key_full, preferred_element_type=jnp.float32)
    value_proj = jnp.dot(normed, value_full, preferred_element_type=jnp.float32)

    def prepare(projected, gain):
        return turn_pairs(
            norm_rows(projected.reshape(tokens, -1, head_width), gain), cosine, sine_part
        )

    queries_f, pull_query = jax.vjp(prepare, query_proj, gain_query)
    keys_f, pull_key = jax.vjp(prepare, key_proj, gain_key)
    queries = queries_f.astype(jnp.bfloat16)
    keys = keys_f[:, 0].astype(jnp.bfloat16)
    values = value_proj.astype(jnp.bfloat16)
    own_pair = jnp.stack([keys, values])
    reach = max(1, WINDOW // tokens)
    moving = own_pair
    received = []
    moving = shifted(moving, "seq", 1)
    received.insert(0, moving)
    every_pair = jnp.concatenate(received + [own_pair], axis=1)
    keys_all = every_pair[0]
    values_all = every_pair[1]
    key_count = keys_all.shape[0]
    distance = (
        jnp.arange(tokens, dtype=jnp.int32)[:, None]
        + reach * tokens
        - jnp.arange(key_count, dtype=jnp.int32)[None, :]
    )
    visible = (distance >= 0) & (distance < WINDOW) & (distance <= offsets[:, None])
    raw_scores = (
        jnp.einsum("thd,kd->htk", queries, keys_all, preferred_element_type=jnp.float32) * scale
    )
    masked = jnp.where(visible[None], raw_scores, masked_value)
    top_score = jnp.max(masked, axis=-1, keepdims=True)
    exponent = jnp.exp(masked - top_score)
    probs = exponent / jnp.sum(exponent, axis=-1, keepdims=True)
    probs_low = probs.astype(jnp.bfloat16)
    attended = jnp.einsum("htk,kd->thd", probs_low, values_all, preferred_element_type=jnp.float32)
    attended = attended.reshape(tokens, heads * head_width).astype(jnp.bfloat16)
    attn_out = jnp.dot(attended, output_full, preferred_element_type=jnp.float32)

    def post_attention(out_value, resid_in, gain_out, gain_next):
        middle_value = resid_in + norm_rows(out_value, gain_out)
        return (middle_value, norm_rows(middle_value, gain_next))

    (middle, ffn_in_f), pull_middle = jax.vjp(
        post_attention, attn_out, inputs, gain_attn, gain_ffn_in
    )
    ffn_in = ffn_in_f.astype(jnp.bfloat16)
    gate_proj = jnp.dot(ffn_in, gate_full, preferred_element_type=jnp.float32)
    upward = jnp.dot(ffn_in, upward_full, preferred_element_type=jnp.float32)

    def activate(gate_value, up_value):
        return jax.nn.gelu(gate_value, approximate=True) * up_value

    hidden_f, pull_act = jax.vjp(activate, gate_proj, upward)
    hidden = hidden_f.astype(jnp.bfloat16)
    ffn_out = jnp.dot(hidden, down_full, preferred_element_type=jnp.float32)

    def finish(ffn_value, middle_value, gain_last):
        return middle_value + norm_rows(ffn_value, gain_last)

    layer_out, pull_out = jax.vjp(finish, ffn_out, middle, gain_ffn_out)
    upstream = cotangent[0].astype(jnp.float32)
    back_ffn_out, back_middle_a, grad_gain_ffn_out = pull_out(upstream)
    back_ffn_low = back_ffn_out.astype(jnp.bfloat16)
    grad_down = jnp.einsum("tf,td->fd", hidden, back_ffn_low, preferred_element_type=jnp.float32)
    back_hidden = jnp.einsum(
        "td,fd->tf", back_ffn_low, down_full, preferred_element_type=jnp.float32
    )
    back_gate, back_upward = pull_act(back_hidden)
    back_gate_low = back_gate.astype(jnp.bfloat16)
    back_up_low = back_upward.astype(jnp.bfloat16)
    grad_gate = jnp.einsum("td,tf->df", ffn_in, back_gate_low, preferred_element_type=jnp.float32)
    grad_up = jnp.einsum("td,tf->df", ffn_in, back_up_low, preferred_element_type=jnp.float32)
    back_ffn_in = jnp.einsum(
        "tf,df->td", back_gate_low, gate_full, preferred_element_type=jnp.float32
    )
    back_ffn_in = back_ffn_in + jnp.einsum(
        "tf,df->td", back_up_low, upward_full, preferred_element_type=jnp.float32
    )
    back_attn_out, back_inputs_a, grad_gain_attn, grad_gain_ffn_in = pull_middle(
        (back_middle_a, back_ffn_in)
    )
    back_attn_low = back_attn_out.astype(jnp.bfloat16)
    grad_output = jnp.einsum(
        "tc,td->cd", attended, back_attn_low, preferred_element_type=jnp.float32
    )
    back_attended = jnp.einsum(
        "td,cd->tc", back_attn_low, output_full, preferred_element_type=jnp.float32
    )
    back_attended = back_attended.reshape(tokens, heads, head_width).astype(jnp.bfloat16)
    back_probs = jnp.einsum(
        "thd,kd->htk", back_attended, values_all, preferred_element_type=jnp.float32
    )
    inner = jnp.sum(probs * back_probs, axis=-1, keepdims=True)
    back_scores = (probs * (back_probs - inner)).astype(jnp.bfloat16)
    back_queries = (
        jnp.einsum("htk,kd->thd", back_scores, keys_all, preferred_element_type=jnp.float32) * scale
    )
    back_keys_all = (
        jnp.einsum("htk,thd->kd", back_scores, queries, preferred_element_type=jnp.float32) * scale
    )
    back_values_all = jnp.einsum(
        "htk,thd->kd", probs_low, back_attended, preferred_element_type=jnp.float32
    )
    grad_pair = jnp.stack([back_keys_all, back_values_all])
    own_part = grad_pair[:, reach * tokens :]
    carried = grad_pair[:, 0 * tokens : (0 + 1) * tokens]
    carried = shifted(carried.astype(jnp.bfloat16), "seq", -1).astype(carried.dtype)
    total_pair = own_part + carried
    back_query_proj, grad_gain_query = pull_query(back_queries)
    back_key_proj, grad_gain_key = pull_key(total_pair[0][:, None, :])
    back_query_low = back_query_proj.astype(jnp.bfloat16)
    back_key_low = back_key_proj.astype(jnp.bfloat16)
    back_value_low = total_pair[1].astype(jnp.bfloat16)
    grad_query = jnp.einsum("td,tc->dc", normed, back_query_low, preferred_element_type=jnp.float32)
    grad_key = jnp.einsum("td,tc->dc", normed, back_key_low, preferred_element_type=jnp.float32)
    grad_value = jnp.einsum("td,tc->dc", normed, back_value_low, preferred_element_type=jnp.float32)
    back_normed = jnp.einsum(
        "tc,dc->td", back_query_low, query_full, preferred_element_type=jnp.float32
    )
    back_normed = back_normed + jnp.einsum(
        "tc,dc->td", back_key_low, key_full, preferred_element_type=jnp.float32
    )
    back_normed = back_normed + jnp.einsum(
        "tc,dc->td", back_value_low, value_full, preferred_element_type=jnp.float32
    )
    back_inputs_b, grad_gain_in = pull_in(back_normed)
    grad_in = (back_inputs_a + back_inputs_b).astype(jnp.bfloat16)
    grads = (
        grad_query,
        grad_key,
        grad_value,
        grad_output,
        grad_gate,
        grad_up,
        grad_down,
        grad_gain_in,
        grad_gain_attn,
        grad_gain_ffn_in,
        grad_gain_ffn_out,
        grad_gain_query,
        grad_gain_key,
    )
    shares = (
        *tuple(
            (
                part.astype(jnp.float32)
                for part in sent_together(
                    (
                        grads[0].astype(jnp.bfloat16),
                        grads[1].astype(jnp.bfloat16),
                        grads[2].astype(jnp.bfloat16),
                    ),
                    "fsdp",
                    0,
                    1,
                )
            )
        ),
        lax.psum_scatter(
            grads[3].astype(jnp.bfloat16), "fsdp", scatter_dimension=0, tiled=True
        ).astype(jnp.float32),
        *tuple(
            (
                part.astype(jnp.float32)
                for part in sent_together(
                    (grads[4].astype(jnp.bfloat16), grads[5].astype(jnp.bfloat16)), "fsdp", 0, 1
                )
            )
        ),
        lax.psum_scatter(
            grads[6].astype(jnp.bfloat16), "fsdp", scatter_dimension=0, tiled=True
        ).astype(jnp.float32),
        lax.psum_scatter(
            grads[7].astype(jnp.bfloat16), "fsdp", scatter_dimension=0, tiled=True
        ).astype(jnp.float32),
        lax.psum_scatter(
            grads[8].astype(jnp.bfloat16), "fsdp", scatter_dimension=0, tiled=True
        ).astype(jnp.float32),
        lax.psum_scatter(
            grads[9].astype(jnp.bfloat16), "fsdp", scatter_dimension=0, tiled=True
        ).astype(jnp.float32),
        lax.psum_scatter(
            grads[10].astype(jnp.bfloat16), "fsdp", scatter_dimension=0, tiled=True
        ).astype(jnp.float32),
        lax.psum_scatter(
            grads[11].astype(jnp.bfloat16), "fsdp", scatter_dimension=0, tiled=True
        ).astype(jnp.float32),
        lax.psum_scatter(
            grads[12].astype(jnp.bfloat16), "fsdp", scatter_dimension=0, tiled=True
        ).astype(jnp.float32),
    )
    totals = (
        lax.psum(shares[0].astype(jnp.bfloat16), "seq").astype(jnp.float32),
        lax.psum(shares[1].astype(jnp.bfloat16), "seq").astype(jnp.float32),
        lax.psum(shares[2].astype(jnp.bfloat16), "seq").astype(jnp.float32),
        lax.psum(shares[3].astype(jnp.bfloat16), "seq").astype(jnp.float32),
        lax.psum(shares[4].astype(jnp.bfloat16), "seq").astype(jnp.float32),
        lax.psum(shares[5].astype(jnp.bfloat16), "seq").astype(jnp.float32),
        lax.psum(shares[6].astype(jnp.bfloat16), "seq").astype(jnp.float32),
        lax.psum(shares[7].astype(jnp.bfloat16), "seq").astype(jnp.float32),
        lax.psum(shares[8].astype(jnp.bfloat16), "seq").astype(jnp.float32),
        lax.psum(shares[9].astype(jnp.bfloat16), "seq").astype(jnp.float32),
        lax.psum(shares[10].astype(jnp.bfloat16), "seq").astype(jnp.float32),
        lax.psum(shares[11].astype(jnp.bfloat16), "seq").astype(jnp.float32),
        lax.psum(shares[12].astype(jnp.bfloat16), "seq").astype(jnp.float32),
    )
    return (layer_out.astype(jnp.bfloat16)[None], grad_in[None]) + tuple(totals)


def solution(mesh):
    placed = (
        P("fsdp", "seq", None),
        P("fsdp", "seq", None),
        P("fsdp", "seq"),
        P("fsdp", None),
        P("fsdp", None),
        P("fsdp", None),
        P("fsdp", None),
        P("fsdp", None),
        P("fsdp", None),
        P("fsdp", None),
        P("fsdp"),
        P("fsdp"),
        P("fsdp"),
        P("fsdp"),
        P("fsdp"),
        P("fsdp"),
    )
    return jax.shard_map(
        body,
        mesh=mesh,
        in_specs=placed,
        out_specs=(
            P("fsdp", "seq", None),
            P("fsdp", "seq", None),
            P("fsdp", None),
            P("fsdp", None),
            P("fsdp", None),
            P("fsdp", None),
            P("fsdp", None),
            P("fsdp", None),
            P("fsdp", None),
            P("fsdp"),
            P("fsdp"),
            P("fsdp"),
            P("fsdp"),
            P("fsdp"),
            P("fsdp"),
        ),
        check_vma=False,
    )
```

profile of v0, /device:TPU:0, one launch (start us, length us, event | category | flops | bytes accessed | tf_op | source)
XLA Modules:
  0.0 747.5 jit_solution(11786712929342229394)
XLA Ops:
  15.4 7.7 %all-reduce.19 = (bf16[640]{0:T(1024)(128)(2,1)S(1)}, bf16[256]{0:T(256)(128)(2,1)S(1)}, bf16[256]{0:T(256)(128)(2,1)S(1)}, bf16[640]{0:T(1024)(128)(2,1)S(1)}, ...) all-reduce(bf16[640]{0:T(1024)(128)(2,1)S(1)} %dynamic-update-slice, ...), channel_id=1, replica_groups=mesh['seq'=32,'fsdp'=4] {'fsdp'}, use_global_device_ids=true, to_apply=%add.4 | all-reduce | flops 3072 | bytes 12288
  26.6 14.1 %all-gather.5.cloned.1.call-done = bf16[640,1536]{1,0:T(8,128)(2,1)} async-done(((bf16[160,1536]{1,0:T(8,128)(2,1)}), bf16[640,1536]{1,0:T(8,128)(2,1)}) %all-gather.5.cloned.1.call-update) | async-done | bytes 1966096 | tf_op jit(solution)/shard_map/all_gather | solution.py:17
  45.2 4.4 collective-permute-start
  55.1 5.5 collective-permute-done
  63.2 6.3 fusion.130
  69.5 4.8 fusion.42
  74.2 3.3 all-gather.7.cloned.1.call-done
  82.6 45.4 %all-gather.9.cloned.1.call-done = bf16[640,4096]{1,0:T(8,128)(2,1)} async-done(((bf16[160,4096]{1,0:T(8,128)(2,1)}), bf16[640,4096]{1,0:T(8,128)(2,1)}) %all-gather.9.cloned.1.call-update) | async-done | bytes 5242896 | tf_op jit(solution)/shard_map/all_gather | solution.py:17
  127.9 3.9 fusion.21
  133.8 4.4 multiply_convert_fusion.1
  138.3 26.1 %all-gather.11.cloned.1.call-done = bf16[2048,640]{1,0:T(8,128)(2,1)} async-done(((bf16[512,640]{1,0:T(8,128)(2,1)}), bf16[2048,640]{1,0:T(8,128)(2,1)}) %all-gather.11.cloned.1.call-update) | async-done | bytes 2621456 | tf_op jit(solution)/shard_map/all_gather | solution.py:69
  164.3 4.4 multiply_reduce_fusion.7
  170.7 4.7 fusion.11
  184.8 2.8 fusion.3
  195.9 13.2 %collective-permute-done.1 = bf16[2,512,256]{1,2,0:T(8,128)(2,1)S(1)} collective-permute-done((bf16[2,512,256]{1,2,0:T(8,128)(2,1)S(1)}, bf16[2,512,256]{1,2,0:T(8,128)(2,1)S(1)}, u32[]{:S(2)}, u32[]{:S(2)}) %collective-permute-start.1) | collective-permute-done | bytes 524320 | tf_op jit(solution)/shard_map/ppermute | solution.py:24
  213.6 3.3 convolution_convert_fusion.1
  224.5 4.9 convolution_convert_fusion
  229.5 15.2 %reduce-scatter.5.cloned.1.call-done = bf16[160,1536]{1,0:T(8,128)(2,1)} async-done(((bf16[640,1536]{1,0:T(8,128)(2,1)}), bf16[160,1536]{1,0:T(8,128)(2,1)}) %reduce-scatter.5.cloned.1.call-update) | async-done | bytes 491536 | tf_op jit(solution)/shard_map/reduce_scatter | solution.py:30
  248.0 53.9 %reduce-scatter.9.cloned.1.call-done = bf16[160,4096]{1,0:T(8,128)(2,1)} async-done(((bf16[640,4096]{1,0:T(8,128)(2,1)}), bf16[160,4096]{1,0:T(8,128)(2,1)}) %reduce-scatter.9.cloned.1.call-update) | async-done | bytes 1310736 | tf_op jit(solution)/shard_map/reduce_scatter | solution.py:30
  304.4 23.3 %reduce-scatter.7.cloned.1.call-done = bf16[256,640]{1,0:T(8,128)(2,1)} async-done(((bf16[1024,640]{1,0:T(8,128)(2,1)}), bf16[256,640]{1,0:T(8,128)(2,1)}) %reduce-scatter.7.cloned.1.call-update) | async-done | bytes 327696 | tf_op jit(solution)/shard_map/reduce_scatter | solution.py:256
  327.8 36.0 %reduce-scatter.11.cloned.1.call-done = bf16[512,640]{1,0:T(8,128)(2,1)} async-done(((bf16[2048,640]{1,0:T(8,128)(2,1)}), bf16[512,640]{1,0:T(8,128)(2,1)}) %reduce-scatter.11.cloned.1.call-update) | async-done | bytes 655376 | tf_op jit(solution)/shard_map/reduce_scatter | solution.py:267
  369.4 6.0 all-reduce.18
  375.9 96.4 %all-reduce.16 = (bf16[160]{0:T(256)(128)(2,1)S(1)}, bf16[160]{0:T(256)(128)(2,1)S(1)}, bf16[160]{0:T(256)(128)(2,1)S(1)}, bf16[160]{0:T(256)(128)(2,1)S(1)}, bf...) all-reduce(bf16[160]{0:T(256)(128)(2,1)S(1)} %dynamic-slice.7, ...), channel_id=1, replica_groups=mesh['seq'=32,'fsdp'=4] {'seq'}, use_global_device_ids=true, to_apply=%region_28.29 | all-reduce | flops 768 | bytes 3072 | tf_op jit(solution)/shard_map/psum | solution.py:297
  476.8 253.4 %all-reduce.22.cloned.1.call-done = (bf16[160,1024]{1,0:T(8,128)(2,1)}, bf16[160,256]{1,0:T(8,128)(2,1)}, bf16[160,256]{1,0:T(8,128)(2,1)}, bf16[256,640]{1,0:T(...) async-done(((bf16[160,1024]{1,0:T(8,128)(2,1)}, bf16[160,256]{1,0:T(8,128)(2,1)}, bf16[160,256]{1,0:T(8,128)(2,1)}, ...) | async-done | bytes 2785296 | tf_op jit(solution)/shard_map/psum | solution.py:290
  (257 shorter events, 86.5 us)
Async XLA Ops:
  7.2 33.5 %all-gather.5.cloned.1.call-start = ((), (), s32[]{:S(2)}) async-start(), calls=%async_computation.4 | async-start | bytes 2457600 | tf_op jit(solution)/shard_map/all_gather | solution.py:17
  9.2 68.3 %all-gather.7.cloned.1.call-start = ((), (), s32[]{:S(2)}) async-start(), calls=%async_computation.5 | async-start | bytes 1638400 | tf_op jit(solution)/shard_map/all_gather | solution.py:67
  10.1 13.0 %copy-start.4 = (bf16[1,512,640]{2,1,0:T(8,128)(2,1)S(1)}, bf16[1,512,640]{2,1,0:T(8,128)(2,1)}, u32[]{:S(2)}) copy-start(bf16[1,512,640]{2,1,0:T(8,128)(2,1)} %param.16) | copy-start | bytes 1966084
  10.1 13.2 %copy-start.41 = (s32[1,512]{1,0:T(1,128)S(1)}, s32[1,512]{1,0:T(1,128)}, u32[]{:S(2)}) copy-start(s32[1,512]{1,0:T(1,128)} %param.18) | copy-start | bytes 6148
  10.1 117.8 %all-gather.9.cloned.1.call-start = ((), (), s32[]{:S(2)}) async-start(), calls=%async_computation.6 | async-start | bytes 6553600 | tf_op jit(solution)/shard_map/all_gather | solution.py:17
  11.3 153.0 %all-gather.11.cloned.1.call-start = ((), (), s32[]{:S(2)}) async-start(), calls=%async_computation.7 | async-start | bytes 3276800 | tf_op jit(solution)/shard_map/all_gather | solution.py:69
  11.9 232.8 %reduce-scatter.5.cloned.1.call-start = ((), (), s32[]{:S(2)}) async-start(), calls=%async_computation.8 | async-start | bytes 2457600 | tf_op jit(solution)/shard_map/reduce_scatter | solution.py:30
  45.2 15.4 %collective-permute-start = (bf16[2,512,256]{1,2,0:T(8,128)(2,1)}, bf16[2,512,256]{1,2,0:T(8,128)(2,1)}, u32[]{:S(2)}, u32[]{:S(2)}) collective-permute-start(bf16[2,512,256]{1,2,0:T(8,128)(2,1)} %pad_maximum_fusion.7), channel_id=1, source_target_pairs={{0,4},{4,8},{8,12},{12,16},{16,20},{20,24},{24,28},{28,32},{32,36}... | collective-permute-start | bytes 1572872 | tf_op jit(solution)/shard_map/ppermute | solution.py:24
  53.9 6.7 copy-start.20
  55.1 8.0 %copy-start.21 = (bf16[512,4,128]{0,2,1:T(8,128)(2,1)}, bf16[512,4,128]{0,2,1:T(8,128)(2,1)S(1)}, u32[]{:S(2)}) copy-start(bf16[512,4,128]{0,2,1:T(8,128)(2,1)S(1)} %get-tuple-element.59) | copy-start | bytes 1572868
  55.1 8.0 %copy-start.23 = (bf16[512,4,128]{0,2,1:T(8,128)(2,1)}, bf16[512,4,128]{0,2,1:T(8,128)(2,1)S(1)}, u32[]{:S(2)}) copy-start(bf16[512,4,128]{0,2,1:T(8,128)(2,1)S(1)} %get-tuple-element.60) | copy-start | bytes 1572868
  61.8 7.7 %copy-start.13 = (bf16[2,1024,256]{1,2,0:T(8,128)(2,1)}, bf16[2,1024,256]{1,2,0:T(8,128)(2,1)S(1)}, u32[]{:S(2)}) copy-start(bf16[2,1024,256]{1,2,0:T(8,128)(2,1)S(1)} %maximum_maximum_fusion) | copy-start | bytes 3145732
  175.4 7.9 %slice-start = ((s8[8388608]{0:T(1024)(128)(4,1)}), s8[4194304]{0:T(1024)(128)(4,1)S(1)}, s32[]{:S(2)}) async-start(s8[8388608]{0:T(1024)(128)(4,1)} %bitcast.183), calls=%async_computation.13 | async-start | bytes 8388608
  192.8 16.4 %collective-permute-start.1 = (bf16[2,512,256]{1,2,0:T(8,128)(2,1)S(1)}, bf16[2,512,256]{1,2,0:T(8,128)(2,1)S(1)}, u32[]{:S(2)}, u32[]{:S(2)}) collective-permute-start(bf16[2,512,256]{1,2,0:T(8,128)(2,1)S(1)} %fusion.73), channel_id=1, source_target_pairs={{4,0},{8,4},{12,8},{16,12},{20,16},{24,20},{28,24},{32,28},{36,32}... | collective-permute-start | bytes 1572872 | tf_op jit(solution)/shard_map/ppermute | solution.py:24
  194.8 14.5 %copy-start.27 = (bf16[512,4,256]{0,2,1:T(8,128)(2,1)}, bf16[512,4,256]{0,2,1:T(8,128)(2,1)S(1)}, u32[]{:S(2)}) copy-start(bf16[512,4,256]{0,2,1:T(8,128)(2,1)S(1)} %fusion.23) | copy-start | bytes 3145732
  213.5 88.4 %reduce-scatter.9.cloned.1.call-start = ((), (), s32[]{:S(2)}) async-start(), calls=%async_computation.10 | async-start | bytes 6553600 | tf_op jit(solution)/shard_map/reduce_scatter | solution.py:30
  221.2 106.6 %reduce-scatter.7.cloned.1.call-start = ((), (), s32[]{:S(2)}) async-start(), calls=%async_computation.9 | async-start | bytes 1638400 | tf_op jit(solution)/shard_map/reduce_scatter | solution.py:256
  224.4 139.3 %reduce-scatter.11.cloned.1.call-start = ((), (), s32[]{:S(2)}) async-start(), calls=%async_computation.11 | async-start | bytes 3276800 | tf_op jit(solution)/shard_map/reduce_scatter | solution.py:267
  229.4 500.8 %all-reduce.22.cloned.1.call-start = ((), (), s32[]{:S(2)}) async-start(), calls=%async_computation.12 | async-start | bytes 5570560 | tf_op jit(solution)/shard_map/psum | solution.py:290
  248.0 117.0 %copy-start.26 = (bf16[640,1536]{1,0:T(8,128)(2,1)S(1)}, bf16[640,1536]{1,0:T(8,128)(2,1)}, u32[]{:S(2)}) copy-start(bf16[640,1536]{1,0:T(8,128)(2,1)} %all-gather.5.cloned.1.call-done) | copy-start | bytes 5898244
  248.0 117.0 %copy-start.28 = (bf16[512,4,256]{0,2,1:T(8,128)(2,1)S(1)}, bf16[512,4,256]{0,2,1:T(8,128)(2,1)}, u32[]{:S(2)}) copy-start(bf16[512,4,256]{0,2,1:T(8,128)(2,1)} %copy-done.27) | copy-start | bytes 3145732
  367.6 108.0 %copy-start.3 = (f32[512,640]{1,0:T(8,128)S(1)}, f32[512,640]{1,0:T(8,128)}, u32[]{:S(2)}) copy-start(f32[512,640]{1,0:T(8,128)} %copy-done.2) | copy-start | bytes 3932164
  730.2 7.0 copy-start.39
  730.3 8.2 %copy-start.38 = (bf16[160,2048]{1,0:T(8,128)(2,1)S(1)}, bf16[160,2048]{1,0:T(8,128)(2,1)}, u32[]{:S(2)}) copy-start(bf16[160,2048]{1,0:T(8,128)(2,1)} %get-tuple-element.38) | copy-start | bytes 1966084
  (51 other events, 155.8 us)
Sparse Core Ops, SparseCore 0:
  10.3 30.4 all-gather.4
  42.4 35.0 all-gather.6
  79.8 48.0 all-gather.8
  129.4 34.8 all-gather.10
  213.6 31.0 reduce-scatter.4
  246.9 54.9 reduce-scatter.8
  304.9 22.8 reduce-scatter.6
  330.2 33.5 reduce-scatter.10
  367.4 362.8 all-reduce.21
where the time goes:
time: 753 us; the launch traced here: 747 us
  waiting for transfers between devices  491 us (65%)
  blocking collectives  110 us (15%)
  matrix products  59.1 us (8%)
  other arithmetic  46.8 us (6%)
  between operations  17.7 us (2%)
  local copies, waits for them, and re-layouts  16.8 us (2%)
    psum x1, waiting for transfers between devices, body(): lax.psum(shares[0].astype(jnp.bfloat16), 'seq').astype(jnp.float32)  253 us
    psum x1, blocking collectives, body(): lax.psum(shares[7].astype(jnp.bfloat16), 'seq').astype(jnp.float32)  96.4 us
    reduce_scatter x2, waiting for transfers between devices, sent_together(): whole = lax.psum_scatter(both, axis, scatter_dimension=dim, tiled=True)  69.1 us
    all_gather x2, waiting for transfers between devices, in_one_piece(): whole = lax.all_gather(both, axis, axis=dim, tiled=True)  59.5 us
    reduce_scatter x1, waiting for transfers between devices, body(): lax.psum_scatter(grads[6].astype(jnp.bfloat16), 'fsdp', scatter_dimension...  36 us
    all_gather x1, waiting for transfers between devices, body(): lax.all_gather(down_weight, 'fsdp', axis=0, tiled=True)  26.1 us
    reduce_scatter x1, waiting for transfers between devices, body(): lax.psum_scatter(grads[3].astype(jnp.bfloat16), 'fsdp', scatter_dimension...  23.3 us
    ppermute x2, waiting for transfers between devices, shifted(): lax.ppermute(value, axis, [(source, source + steps) for source in range(f...  18.7 us
  transfers between devices with their start and end apart: 11, of which 11 were waited for; matrix products, arithmetic and copies ran while one was open for 10% of the time, Pallas kernels for 0%

commit v1 on v0

v1 whole, which is shorter than its diff:
```python
import jax
import jax.numpy as jnp
from jax import lax
from jax.sharding import PartitionSpec as P

WINDOW = 512
epsilon = 1e-06
rope_base = 10000.0
masked_value = -1e30
bf16 = jnp.bfloat16
f32 = jnp.float32


def seq_index(z, x, y):
    return (z % 2 * 4 + x % 4) * 4 + y % 4


def along_xy(dx, dy):
    return [
        (seq_index(z, x, y), seq_index(z, x + dx, y + dy))
        for z in range(2)
        for x in range(4)
        for y in range(4)
    ]


def along_z(step):
    pairs = []
    for s in range(32):
        for f in range(4):
            z = s // 16 * 2 + f // 2
            t = step(z)
            pairs.append((s * 4 + f, (t // 2 * 16 + s % 16) * 4 + t % 2 * 2 + f % 2))
    return pairs


def swap_core(value):
    return lax.ppermute(value, "fsdp", [(0, 1), (1, 0), (2, 3), (3, 2)])


def swap_near(value):
    return lax.ppermute(value, "fsdp", [(0, 2), (1, 3), (2, 0), (3, 1)])


def swap_far(value):
    return lax.ppermute(value, ("seq", "fsdp"), along_z(lambda z: 3 - z))


def swap_hi(value):
    return lax.ppermute(value, "seq", [(s, (s + 16) % 32) for s in range(32)])


def move_x(value, d):
    return lax.ppermute(value, "seq", along_xy(d, 0))


def move_y(value, d):
    return lax.ppermute(value, "seq", along_xy(0, d))


def shifted(value, steps):
    first, last = (max(0, -steps), min(32, 32 - steps))
    return lax.ppermute(value, "seq", [(source, source + steps) for source in range(first, last)])


def pick(value, index, axis):
    return lax.dynamic_index_in_dim(value, index, axis, keepdims=False)


def total(parts):
    whole = parts[0].astype(f32)
    for part in parts[1:]:
        whole = whole + part.astype(f32)
    return whole.astype(bf16)


def in_order(pieces, me, sign):
    stack = jnp.stack(pieces)
    return jnp.stack([pick(stack, (sign * (me - j)) % 4, 0) for j in range(4)])


def reduce_group(buf, x, y, z_lo, core):
    rows = buf.shape[2]
    got = swap_core(pick(buf, 1 - core, 1))
    half = total([pick(buf, core, 1), got]).reshape(2, 2, 4, 4, rows // 32, 128)
    a, b = half[:, 0], half[:, 1]
    steps = (1, 3, 2)
    from_a = [move_x(pick(a, (x + d) % 4, 1), d) for d in steps]
    from_b = [move_y(pick(b, (y + d) % 4, 1), d) for d in steps]
    a = total([pick(a, x, 1)] + from_a)
    b = total([pick(b, y, 1)] + from_b)
    from_a = [move_y(pick(a, (y + d) % 4, 1), d) for d in steps]
    from_b = [move_x(pick(b, (x + d) % 4, 1), d) for d in steps]
    a = total([pick(a, y, 1)] + from_a)
    b = total([pick(b, x, 1)] + from_b)
    both = jnp.stack([a, b], axis=1)
    mine = pick(both, z_lo, 0)
    other = pick(both, 1 - z_lo, 0)
    both = total([mine, swap_near(other), swap_far(other), swap_hi(mine)])
    a, b = both[0], both[1]
    a = in_order([a] + [move_y(a, d) for d in (1, 2, 3)], y, 1)
    b = in_order([b] + [move_x(b, d) for d in (1, 2, 3)], x, 1)
    a = in_order([a] + [move_x(a, d) for d in (1, 2, 3)], x, 1)
    b = in_order([b] + [move_y(b, d) for d in (1, 2, 3)], y, 1)
    return jnp.stack([a, b]).reshape(rows, 128)


def blocks_of(grad):
    r, c = grad.shape[0] // 4, grad.shape[1]
    return grad.reshape(4, r, c // 128, 128).transpose(0, 2, 1, 3).reshape(4, r * c // 128, 128)


def from_blocks(flat, r, c):
    return flat.reshape(c // 128, r, 128).transpose(1, 0, 2).reshape(r, c).astype(f32)


def norm_rows(values, gain):
    return values * lax.rsqrt(jnp.mean(values * values, axis=-1, keepdims=True) + epsilon) * gain


def turn_pairs(values, cosine, sine_part):
    half_width = values.shape[-1] // 2
    leading = values[..., :half_width]
    trailing = values[..., half_width:]
    return jnp.concatenate(
        [leading * cosine - trailing * sine_part, trailing * cosine + leading * sine_part], axis=-1
    )


def dot(a, b, dims):
    return lax.dot_general(a, b, (dims, ((), ())), preferred_element_type=f32)


def body(
    hidden_in,
    cotangent,
    positions,
    query_weight,
    key_weight,
    value_weight,
    output_weight,
    gate_weight,
    up_weight,
    down_weight,
    norm_in,
    norm_attn,
    norm_ffn_in,
    norm_ffn_out,
    norm_query,
    norm_key,
):
    s = lax.axis_index("seq")
    f = lax.axis_index("fsdp")
    x, y, z_lo, core = s // 4 % 4, s % 4, f // 2, f % 2
    gains = jnp.concatenate(
        [norm_in, norm_attn, norm_ffn_in, norm_ffn_out, norm_query, norm_key]
    )
    gains = jnp.pad(gains, (0, 8 * 512 - gains.shape[0])).reshape(8, 512)
    kvg = jnp.concatenate([jnp.concatenate([key_weight, value_weight], axis=1), gains], axis=0)

    def everywhere(own, swap):
        partner = swap(own)
        sibling = swap_core(own)
        diagonal = swap_core(partner)
        out = []
        for j in range(4):
            low = jnp.where(j % 2 == core, own, sibling)
            high = jnp.where(j % 2 == core, partner, diagonal)
            out.append(jnp.where(j // 2 == z_lo, low, high))
        return out

    query_full = jnp.concatenate(everywhere(query_weight, swap_near))
    kvg_parts = everywhere(kvg, swap_far)
    halo = shifted(hidden_in[0], 1)
    output_full = jnp.concatenate(everywhere(output_weight, swap_near))
    gate_full = jnp.concatenate(everywhere(gate_weight, swap_near))
    upward_full = jnp.concatenate(everywhere(up_weight, swap_far))
    down_full = jnp.concatenate(everywhere(down_weight, swap_far))
    kv_full = jnp.concatenate([part[:160] for part in kvg_parts])
    gain_rows = jnp.stack([part[160:162] for part in kvg_parts]).reshape(4, 1024).astype(f32)
    gain_in, gain_attn, gain_ffn_in, gain_ffn_out = [
        gain_rows[:, 160 * k : 160 * (k + 1)].reshape(640) for k in range(4)
    ]
    gain_query, gain_key = [
        gain_rows[:, 640 + 64 * k : 704 + 64 * k].reshape(256) for k in range(2)
    ]

    inputs = hidden_in[0].astype(f32)
    offsets = positions[0]
    tokens = inputs.shape[0]
    head_width = 256
    heads = 4
    half_width = head_width // 2
    scale = head_width ** (-0.5)
    powers = jnp.arange(half_width, dtype=f32) * (2.0 / head_width)
    row = jnp.arange(tokens, dtype=jnp.int32)
    offsets_all = jnp.concatenate([offsets[0] - tokens + row, offsets])
    angles = offsets_all.astype(f32)[:, None] * (rope_base ** (-powers))[None, :]
    cosine = jnp.cos(angles)[:, None, :]
    sine_part = jnp.sin(angles)[:, None, :]
    inputs_all = jnp.concatenate([halo, hidden_in[0]]).astype(f32)
    normed_f, pull_in = jax.vjp(norm_rows, inputs_all, gain_in)
    normed_all = normed_f.astype(bf16)
    normed = normed_all[tokens:]
    query_proj = dot(normed, query_full, ((1,), (0,)))
    kv_proj = dot(normed_all, kv_full, ((1,), (0,)))
    key_proj = kv_proj[:, :head_width]
    values_all = kv_proj[:, head_width:].astype(bf16)

    def prepare(projected, gain, cosine, sine_part):
        return turn_pairs(
            norm_rows(projected.reshape(projected.shape[0], -1, head_width), gain),
            cosine,
            sine_part,
        )

    queries_f, pull_query = jax.vjp(
        lambda p, g: prepare(p, g, cosine[tokens:], sine_part[tokens:]), query_proj, gain_query
    )
    keys_f, pull_key = jax.vjp(
        lambda p, g: prepare(p, g, cosine, sine_part), key_proj, gain_key
    )
    queries = queries_f.astype(bf16)
    keys_all = keys_f[:, 0].astype(bf16)
    distance = row[:, None] + tokens - jnp.arange(2 * tokens, dtype=jnp.int32)[None, :]
    visible = (distance >= 0) & (distance < WINDOW) & (distance <= offsets[:, None])
    raw_scores = jnp.einsum("thd,kd->htk", queries, keys_all, preferred_element_type=f32) * scale
    masked = jnp.where(visible[None], raw_scores, masked_value)
    top_score = jnp.max(masked, axis=-1, keepdims=True)
    exponent = jnp.exp(masked - top_score)
    probs = exponent / jnp.sum(exponent, axis=-1, keepdims=True)
    probs_low = probs.astype(bf16)
    attended = jnp.einsum("htk,kd->thd", probs_low, values_all, preferred_element_type=f32)
    attended = attended.reshape(tokens, heads * head_width).astype(bf16)
    attn_out = dot(attended, output_full, ((1,), (0,)))

    def post_attention(out_value, resid_in, gain_out, gain_next):
        middle_value = resid_in + norm_rows(out_value, gain_out)
        return (middle_value, norm_rows(middle_value, gain_next))

    (middle, ffn_in_f), pull_middle = jax.vjp(
        post_attention, attn_out, inputs, gain_attn, gain_ffn_in
    )
    ffn_in = ffn_in_f.astype(bf16)
    gate_proj = dot(ffn_in, gate_full, ((1,), (0,)))
    upward = dot(ffn_in, upward_full, ((1,), (0,)))

    def activate(gate_value, up_value):
        return jax.nn.gelu(gate_value, approximate=True) * up_value

    hidden_f, pull_act = jax.vjp(activate, gate_proj, upward)
    hidden = hidden_f.astype(bf16)
    ffn_out = dot(hidden, down_full, ((1,), (0,)))

    def finish(ffn_value, middle_value, gain_last):
        return middle_value + norm_rows(ffn_value, gain_last)

    layer_out, pull_out = jax.vjp(finish, ffn_out, middle, gain_ffn_out)
    upstream = cotangent[0].astype(f32)
    back_ffn_out, back_middle_a, grad_gain_ffn_out = pull_out(upstream)
    back_ffn_low = back_ffn_out.astype(bf16)
    grad_down = dot(hidden, back_ffn_low, ((0,), (0,))).astype(bf16)
    back_hidden = dot(back_ffn_low, down_full, ((1,), (1,)))
    back_gate, back_upward = pull_act(back_hidden)
    back_gate_low = back_gate.astype(bf16)
    back_up_low = back_upward.astype(bf16)
    grad_gate = dot(ffn_in, back_gate_low, ((0,), (0,))).astype(bf16)
    grad_up = dot(ffn_in, back_up_low, ((0,), (0,))).astype(bf16)
    ffn_buf = jnp.concatenate([blocks_of(g) for g in (grad_gate, grad_up, grad_down)], axis=1)
    ffn_total = reduce_group(ffn_buf.reshape(2, 2, -1, 128), x, y, z_lo, core)

    back_ffn_in = dot(back_gate_low, gate_full, ((1,), (1,)))
    back_ffn_in = back_ffn_in + dot(back_up_low, upward_full, ((1,), (1,)))
    back_attn_out, back_inputs_a, grad_gain_attn, grad_gain_ffn_in = pull_middle(
        (back_middle_a, back_ffn_in)
    )
    back_attn_low = back_attn_out.astype(bf16)
    grad_output = dot(attended, back_attn_low, ((0,), (0,))).astype(bf16)
    back_attended = dot(back_attn_low, output_full, ((1,), (1,)))
    back_attended = back_attended.reshape(tokens, heads, head_width).astype(bf16)
    back_probs = jnp.einsum("thd,kd->htk", back_attended, values_all, preferred_element_type=f32)
    inner = jnp.sum(probs * back_probs, axis=-1, keepdims=True)
    back_scores = (probs * (back_probs - inner)).astype(bf16)
    back_queries = (
        jnp.einsum("htk,kd->thd", back_scores, keys_all, preferred_element_type=f32) * scale
    )
    back_keys_all = (
        jnp.einsum("htk,thd->kd", back_scores, queries, preferred_element_type=f32) * scale
    )
    back_values_all = jnp.einsum(
        "htk,thd->kd", probs_low, back_attended, preferred_element_type=f32
    )
    back_key_proj, grad_gain_key = pull_key(back_keys_all[:, None, :])
    back_kv_low = jnp.concatenate([back_key_proj, back_values_all], axis=1).astype(bf16)
    back_normed_kv = dot(back_kv_low, kv_full, ((1,), (1,)))
    returned = shifted(back_normed_kv[:tokens].astype(bf16), -1)
    back_query_proj, grad_gain_query = pull_query(back_queries)
    back_query_low = back_query_proj.astype(bf16)
    grad_query = dot(normed, back_query_low, ((0,), (0,))).astype(bf16)
    grad_kv = dot(normed_all, back_kv_low, ((0,), (0,))).astype(bf16)
    back_normed = back_normed_kv[tokens:] + dot(back_query_low, query_full, ((1,), (1,)))
    _, grad_gain_in = pull_in(jnp.concatenate([back_normed_kv[:tokens], back_normed]))
    gain_grads = jnp.concatenate(
        [
            g.reshape(4, -1)
            for g in (
                grad_gain_in,
                grad_gain_attn,
                grad_gain_ffn_in,
                grad_gain_ffn_out,
                grad_gain_query,
                grad_gain_key,
            )
        ],
        axis=1,
    ).astype(bf16)
    gain_grads = jnp.pad(gain_grads, ((0, 0), (0, 128 * 128 - 768))).reshape(4, 128, 128)
    attn_buf = jnp.concatenate(
        [blocks_of(g) for g in (grad_query, grad_kv, grad_output)] + [gain_grads], axis=1
    )
    attn_total = reduce_group(attn_buf.reshape(2, 2, -1, 128), x, y, z_lo, core)
    _, pull_own = jax.vjp(norm_rows, inputs, gain_in)
    back_inputs_b, _ = pull_own(back_normed + returned.astype(f32))
    grad_in = (back_inputs_a + back_inputs_b).astype(bf16)

    gain_total = attn_total[3200:3206].reshape(768).astype(f32)
    kv_total = from_blocks(attn_total[1280:1920], 160, 512)
    return (
        layer_out.astype(bf16)[None],
        grad_in[None],
        from_blocks(attn_total[:1280], 160, 1024),
        kv_total[:, :256],
        kv_total[:, 256:],
        from_blocks(attn_total[1920:3200], 256, 640),
        from_blocks(ffn_total[:2560], 160, 2048),
        from_blocks(ffn_total[2560:5120], 160, 2048),
        from_blocks(ffn_total[5120:], 512, 640),
        gain_total[:160],
        gain_total[160:320],
        gain_total[320:480],
        gain_total[480:640],
        gain_total[640:704],
        gain_total[704:768],
    )


def solution(mesh):
    three = P("fsdp", "seq", None)
    two = P("fsdp", None)
    one = P("fsdp")
    return jax.shard_map(
        body,
        mesh=mesh,
        in_specs=(three, three, P("fsdp", "seq")) + (two,) * 7 + (one,) * 6,
        out_specs=(three, three) + (two,) * 7 + (one,) * 6,
        check_vma=False,
    )
```

time: 753 us -> 370 us (0.49)
  waiting for transfers between devices: 491 us -> 82.2 us
  blocking collectives: 110 us -> 0 us
  starting transfers between devices: 6.33 us -> 103 us
  local copies, waits for them, and re-layouts: 16.8 us -> 60 us
  between operations: 17.7 us -> 3.76 us
    psum x1 -> x0, waiting for transfers between devices: 253 us -> none  [body(): lax.psum(shares[0].astype(jnp.bfloat16), 'seq').astype(jnp.float32)]
    reduce_scatter x4 -> x0, waiting for transfers between devices: 128 us -> none  [the longest x2 69.1 us: sent_together(): whole = lax.psum_scatter(both, axis, scatter_dimension=dim, tiled=True)]
    ppermute x2 -> x76, starting transfers between devices: 5.8 us -> 103 us  [the longest x24 37.6 us: move_x(): return lax.ppermute(value, 'seq', along_xy(d, 0))]
    psum x1 -> x0, blocking collectives: 96.4 us -> none  [body(): lax.psum(shares[7].astype(jnp.bfloat16), 'seq').astype(jnp.float32)]
    all_gather x4 -> x0, waiting for transfers between devices: 88.8 us -> none  [the longest x2 59.5 us: in_one_piece(): whole = lax.all_gather(both, axis, axis=dim, tiled=True)]
    ppermute x2 -> x76, waiting for transfers between devices: 18.7 us -> 82.2 us  [the longest x24 35.6 us: move_x(): return lax.ppermute(value, 'seq', along_xy(d, 0))]
    unnamed x2 -> x0, blocking collectives: 13.7 us -> none
    reshape x0 -> x15, local copies, waits for them, and re-layouts: none -> 12.5 us  [the longest x7 9.96 us: blocks_of(): grad.reshape(4, r, c // 128, 128).transpose(0, 2, 1, 3)]
  transfers between devices with their start and end apart: 11 -> 76, of which waited for: 11 -> 26; matrix products, arithmetic and copies ran while one was open for 10% -> 26% of each run, Pallas kernels for 0% -> 0%
where the time goes in v1:
time: 370 us; the launch traced here: 363 us
  starting transfers between devices  103 us (28%)
  waiting for transfers between devices  82.2 us (22%)
  matrix products  63.6 us (17%)
  local copies, waits for them, and re-layouts  60 us (16%)
  other arithmetic  51.2 us (14%)
  between operations  3.76 us (1%)
    dot_general x18, matrix products, dot(): return lax.dot_general(a, b, (dims, ((), ())), preferred_element_type=f32)  44.6 us
    ppermute x24, starting transfers between devices, move_x(): return lax.ppermute(value, 'seq', along_xy(d, 0))  37.6 us
    ppermute x24, waiting for transfers between devices, move_x(): return lax.ppermute(value, 'seq', along_xy(d, 0))  35.6 us
    ppermute x24, starting transfers between devices, move_y(): return lax.ppermute(value, 'seq', along_xy(0, d))  35 us
    ppermute x5, waiting for transfers between devices, swap_far(): return lax.ppermute(value, ('seq', 'fsdp'), along_z(lambda z: 3 - z))  25.4 us
    unnamed x177, local copies, waits for them, and re-layouts  15.1 us
    ppermute x5, starting transfers between devices, swap_far(): return lax.ppermute(value, ('seq', 'fsdp'), along_z(lambda z: 3 - z))  12.5 us
    reshape x7, local copies, waits for them, and re-layouts, blocks_of(): grad.reshape(4, r, c // 128, 128).transpose(0, 2, 1, 3)  9.96 us
  transfers between devices with their start and end apart: 76, of which 26 were waited for; matrix products, arithmetic and copies ran while one was open for 26% of the time, Pallas kernels for 0%

profile of v1, /device:TPU:0, one launch (start us, length us, event | category | flops | bytes accessed | tf_op | source)
XLA Modules:
  0.0 363.4 jit_solution(12120399486854728020)
XLA Ops:
  0.7 4.2 %concatenate.81 = bf16[768]{0:T(1024)(128)(2,1)S(1)} concatenate(bf16[160]{0:T(256)(128)(2,1)} %param.26, bf16[160]{0:T(256)(128)(2,1)} %param.27, bf16[160]{0:T(256)(128)(2,1)} %param.28, bf16[160]{0:T(256)(128)(2,1)} %param.29, bf16[64]{0:T(256)(128)(2,1)} %param.30, bf16[64]{0:T(256)(128)(2,1)} %param.31), dimensions={0} | concatenate | bytes 3072 | tf_op jit(solution)/shard_map/concatenate | solution.py:155
  5.9 4.2 %collective-permute-start.2 = (bf16[168,512]{1,0:T(8,128)(2,1)S(1)}, bf16[168,512]{1,0:T(8,128)(2,1)S(1)}, u32[]{:S(2)}, u32[]{:S(2)}) collective-permute-start(bf16[168,512]{1,0:T(8,128)(2,1)S(1)} %pad_maximum_fusion.35), channel_id=1, source_target_pairs={{0,66},{1,67},{2,64},{3,65},{4,70},{5,71},{6,68},{7,69},{8,74},{9,... | collective-permute-start | bytes 516104 | tf_op jit(solution)/shard_map/ppermute | solution.py:46
  19.2 3.5 collective-permute-start
  30.3 6.4 %collective-permute-done = bf16[512,640]{1,0:T(8,128)(2,1)S(1)} collective-permute-done((bf16[512,640]{1,0:T(8,128)(2,1)S(1)}, bf16[512,640]{1,0:T(8,128)(2,1)S(1)}, u32[]{:S(2)}, u32[]{:S(2)}) %collective-permute-start) | collective-permute-done | bytes 655392 | tf_op jit(solution)/shard_map/ppermute | solution.py:63
  38.0 3.7 %collective-permute-done.8 = bf16[256,640]{1,0:T(8,128)(2,1)} collective-permute-done((bf16[256,640]{1,0:T(8,128)(2,1)S(1)}, bf16[256,640]{1,0:T(8,128)(2,1)}, u32[]{:S(2)}, u32[]{:S(2)}) %collective-permute-start.8) | collective-permute-done | bytes 327712 | tf_op jit(solution)/shard_map/ppermute | solution.py:42
  58.6 6.3 %fusion.169 = (f32[4,512]{1,0:T(4,128)S(1)}, f32[4,512,1024]{1,2,0:T(8,128)}) fusion(f32[1024,512,4]{1,0,2:T(8,128)S(1)} %fusion.76, pred[512,1024]{0,1:T(8,128)(4,1)S(1)} %copy-done.30), kind=kOutput, calls=%fused_computation.437 | output fusion | flops 12583935 | bytes 17309696 | tf_op jit(solution)/shard_map/sub | solution.py:230
  64.9 4.8 %fusion.38 = bf16[256,4,512]{2,0,1:T(8,128)(2,1)S(1)} fusion(f32[1024,512]{0,1:T(8,128)S(1)} %fusion.117, f32[4,512,1024]{1,2,0:T(8,128)} %get-tuple-element.247, f32[4,512]{1,0:T(4,128)S(1)} %get-tuple-element.246), kind=kOutput, calls=%fused_computation.86 | convolution fusion | flops 1078460416 | bytes 9969664 | tf_op jit(solution)/shard_map/htk,kd->thd/dot_general | solution.py:233
  69.7 4.9 %collective-permute-start.14 = (bf16[160,2048]{1,0:T(8,128)(2,1)}, bf16[160,2048]{1,0:T(8,128)(2,1)S(1)}, u32[]{:S(2)}, u32[]{:S(2)}) collective-permute-start(bf16[160,2048]{1,0:T(8,128)(2,1)} %param.24), channel_id=1, source_target_pairs={{0,66},{1,67},{2,64},{3,65},{4,70},{5,71},{6,68},{7,69},{8,74},{9,... | collective-permute-start | bytes 1966088 | tf_op jit(solution)/shard_map/ppermute | solution.py:46
  78.5 11.8 %collective-permute-done.14 = bf16[160,2048]{1,0:T(8,128)(2,1)S(1)} collective-permute-done((bf16[160,2048]{1,0:T(8,128)(2,1)}, bf16[160,2048]{1,0:T(8,128)(2,1)S(1)}, u32[]{:S(2)}, u32[]{:S(2)}) %collective-permute-start.14) | collective-permute-done | bytes 655392 | tf_op jit(solution)/shard_map/ppermute | solution.py:46
  90.3 13.7 %collective-permute-done.17 = bf16[512,640]{1,0:T(8,128)(2,1)S(1)} collective-permute-done((bf16[512,640]{1,0:T(8,128)(2,1)S(1)}, bf16[512,640]{1,0:T(8,128)(2,1)S(1)}, u32[]{:S(2)}, u32[]{:S(2)}) %collective-permute-start.17) | collective-permute-done | bytes 655392 | tf_op jit(solution)/shard_map/ppermute | solution.py:46
  118.1 9.7 %fusion.12 = (bf16[512,2048]{1,0:T(8,128)(2,1)S(1)}, bf16[512,2048]{1,0:T(8,128)(2,1)S(1)}) fusion(f32[512,2048]{1,0:T(8,128)S(1)} %fusion.94, f32[512,2048]{1,0:T(8,128)S(1)} %get-tuple-element.251, bf16[512,640]{1,0:T(8,128)(2,1)S(1)} %get-tuple-element.137, bf16[512,640]{1,0:T(8,128)(2,1)S(1)} %get-tuple-element.112, ...), kind=kOutput, calls=%fused_computation.20 | convolution fusion | flops 1377828864 | bytes 15859712 | tf_op jit(solution)/shard_map/dot_general | solution.py:131
  140.3 5.1 %fusion.55 = bf16[1024,256]{0,1:T(8,128)(2,1)S(1)} fusion(bf16[512,4,256]{0,2,1:T(8,128)(2,1)} %bitcast.417, f32[4,512,1024]{1,2,0:T(8,128)} %get-tuple-element.247, f32[4,512]{1,0:T(4,128)} %copy-done.63), kind=kOutput, calls=%fused_computation.122 | convolution fusion | flops 1078198272 | bytes 9969664 | tf_op jit(solution)/shard_map/htk,thd->kd/dot_general | solution.py:290
  145.4 4.8 %fusion.1 = (f32[4,512]{1,0:T(4,128)S(1)}, f32[1024,512,4]{1,0,2:T(8,128)S(1)}) fusion(f32[4,512,1024]{1,2,0:T(8,128)} %get-tuple-element.247, f32[4,512]{1,0:T(4,128)S(1)} %copy-done.64, bf16[512,4,256]{0,2,1:T(8,128)(2,1)S(1)} %bitcast.418, f32[1024,512]{0,1:T(8,128)S(1)} %copy-done.4), kind=kOutput, calls=%fused_computation.3 | convolution fusion | flops 1080031232 | bytes 18366464 | tf_op jit(solution)/shard_map/thd,kd->htk/dot_general | solution.py:281
  150.2 4.4 %fusion.3 = bf16[4,512,1024]{1,2,0:T(8,128)(2,1)S(1)} fusion(f32[1024,512,4]{1,0,2:T(8,128)S(1)} %get-tuple-element.256, f32[4,512]{1,0:T(4,128)S(1)} %get-tuple-element.255, f32[4,512,1024]{1,2,0:T(8,128)} %get-tuple-element.247, f32[4,512]{1,0:T(4,128)S(1)} %copy-done.64), kind=kLoop, calls=%fused_computation.5 | loop fusion | flops 8388608 | bytes 20987904 | tf_op jit(solution)/shard_map/convert_element_type | solution.py:283
  191.8 3.6 reshape.556
  195.4 4.4 %copy.202 = bf16[4,5,512,128]{3,2,1,0:T(8,128)(2,1)S(1)} copy(bf16[4,5,512,128]{2,0,3,1:T(4,128)(2,1)} %bitcast.392) | data formatting | bytes 5242880 | tf_op jit(solution)/shard_map/transpose | solution.py:110
  199.9 3.6 fusion.53
  223.2 4.0 %collective-permute-done.23 = bf16[2,4,104,128]{3,2,0,1:T(8,128)(2,1)S(1)} collective-permute-done((bf16[2,4,104,128]{3,2,0,1:T(8,128)(2,1)S(1)}, bf16[2,4,104,128]{3,2,0,1:T(8,128)(2,1)S(1)}, u32[]{:S(2)}, u32[]{:S(2)}) %collective-permute-start.23) | collective-permute-done | bytes 213024 | tf_op jit(solution)/shard_map/ppermute | solution.py:54
  227.3 3.4 collective-permute-done.22
  232.9 3.8 %collective-permute-start.25 = (bf16[2,104,128]{2,1,0:T(8,128)(2,1)S(1)}, bf16[2,104,128]{2,1,0:T(8,128)(2,1)S(1)}, u32[]{:S(2)}, u32[]{:S(2)}) collective-permute-start(bf16[2,104,128]{2,1,0:T(8,128)(2,1)S(1)} %get-tuple-element.209), channel_id=1, source_target_pairs={{0,12},{4,0},{8,4},{12,8},{16,28},{20,16},{24,20},{28,24},{32,44},... | collective-permute-start | bytes 159752 | tf_op jit(solution)/shard_map/ppermute | solution.py:58
  284.4 6.6 %collective-permute-start.51 = (bf16[2,4,240,128]{3,2,0,1:T(8,128)(2,1)S(1)}, bf16[2,4,240,128]{3,2,0,1:T(8,128)(2,1)S(1)}, u32[]{:S(2)}, u32[]{:S(2)}) collective-permute-start(bf16[2,4,240,128]{3,2,0,1:T(8,128)(2,1)S(1)} %bitcast.423), channel_id=1, source_target_pairs={{0,32},{4,36},{8,40},{12,44},{16,48},{20,52},{24,56},{28,60},{32,0... | collective-permute-start | bytes 1474568 | tf_op jit(solution)/shard_map/ppermute | solution.py:54
  301.4 4.3 %collective-permute-done.49 = bf16[2,4,240,128]{3,2,0,1:T(8,128)(2,1)S(1)} collective-permute-done((bf16[2,4,240,128]{3,2,0,1:T(8,128)(2,1)S(1)}, bf16[2,4,240,128]{3,2,0,1:T(8,128)(2,1)S(1)}, u32[]{:S(2)}, u32[]{:S(2)}) %collective-permute-start.49) | collective-permute-done | bytes 491552 | tf_op jit(solution)/shard_map/ppermute | solution.py:54
  306.0 5.2 %collective-permute-start.54 = (bf16[2,240,128]{2,1,0:T(8,128)(2,1)S(1)}, bf16[2,240,128]{2,1,0:T(8,128)(2,1)S(1)}, u32[]{:S(2)}, u32[]{:S(2)}) collective-permute-start(bf16[2,240,128]{2,1,0:T(8,128)(2,1)S(1)} %get-tuple-element.178), channel_id=1, source_target_pairs={{0,8},{4,12},{8,0},{12,4},{16,24},{20,28},{24,16},{28,20},{32,40},... | collective-permute-start | bytes 368648 | tf_op jit(solution)/shard_map/ppermute | solution.py:58
  328.3 3.9 %collective-permute-done.63 = bf16[2,240,128]{2,1,0:T(8,128)(2,1)S(1)} collective-permute-done((bf16[2,240,128]{2,1,0:T(8,128)(2,1)S(1)}, bf16[2,240,128]{2,1,0:T(8,128)(2,1)S(1)}, u32[]{:S(2)}, u32[]{:S(2)}) %collective-permute-start.63) | collective-permute-done | bytes 122912 | tf_op jit(solution)/shard_map/ppermute | solution.py:50
  (492 shorter events, 229.4 us)
Async XLA Ops:
  5.8 11.3 %collective-permute-start.1 = (bf16[168,512]{1,0:T(8,128)(2,1)S(1)}, bf16[168,512]{1,0:T(8,128)(2,1)S(1)}, u32[]{:S(2)}, u32[]{:S(2)}) collective-permute-start(bf16[168,512]{1,0:T(8,128)(2,1)S(1)} %pad_maximum_fusion.35), channel_id=1, source_target_pairs={{0,1},{1,0},{2,3},{3,2},{4,5},{5,4},{6,7},{7,6},{8,9},{9,8},{10,11... | collective-permute-start | bytes 516104 | tf_op jit(solution)/shard_map/ppermute | solution.py:38
  10.1 27.3 %collective-permute-start.4 = (bf16[160,1024]{1,0:T(8,128)(2,1)}, bf16[160,1024]{1,0:T(8,128)(2,1)S(1)}, u32[]{:S(2)}, u32[]{:S(2)}) collective-permute-start(bf16[160,1024]{1,0:T(8,128)(2,1)} %param.19), channel_id=1, source_target_pairs={{0,1},{1,0},{2,3},{3,2},{4,5},{5,4},{6,7},{7,6},{8,9},{9,8},{10,11... | collective-permute-start | bytes 983048 | tf_op jit(solution)/shard_map/ppermute | solution.py:38
  10.3 20.0 %collective-permute-start.5 = (bf16[160,1024]{1,0:T(8,128)(2,1)}, bf16[160,1024]{1,0:T(8,128)(2,1)}, u32[]{:S(2)}, u32[]{:S(2)}) collective-permute-start(bf16[160,1024]{1,0:T(8,128)(2,1)} %param.19), channel_id=1, source_target_pairs={{0,2},{1,3},{2,0},{3,1},{4,6},{5,7},{6,4},{7,5},{8,10},{9,11},{10,... | collective-permute-start | bytes 983048 | tf_op jit(solution)/shard_map/ppermute | solution.py:42
  10.3 59.4 %collective-permute-start.7 = (bf16[256,640]{1,0:T(8,128)(2,1)}, bf16[256,640]{1,0:T(8,128)(2,1)}, u32[]{:S(2)}, u32[]{:S(2)}) collective-permute-start(bf16[256,640]{1,0:T(8,128)(2,1)} %param.22), channel_id=1, source_target_pairs={{0,1},{1,0},{2,3},{3,2},{4,5},{5,4},{6,7},{7,6},{8,9},{9,8},{10,11... | collective-permute-start | bytes 983048 | tf_op jit(solution)/shard_map/ppermute | solution.py:38
  17.1 24.6 %collective-permute-start.8 = (bf16[256,640]{1,0:T(8,128)(2,1)S(1)}, bf16[256,640]{1,0:T(8,128)(2,1)}, u32[]{:S(2)}, u32[]{:S(2)}) collective-permute-start(bf16[256,640]{1,0:T(8,128)(2,1)S(1)} %copy-done.32), channel_id=1, source_target_pairs={{0,2},{1,3},{2,0},{3,1},{4,6},{5,7},{6,4},{7,5},{8,10},{9,11},{10,... | collective-permute-start | bytes 983048 | tf_op jit(solution)/shard_map/ppermute | solution.py:42
  19.2 17.4 %collective-permute-start = (bf16[512,640]{1,0:T(8,128)(2,1)S(1)}, bf16[512,640]{1,0:T(8,128)(2,1)S(1)}, u32[]{:S(2)}, u32[]{:S(2)}) collective-permute-start(bf16[512,640]{1,0:T(8,128)(2,1)S(1)} %bitcast.387), channel_id=1, source_target_pairs={{0,4},{4,8},{8,12},{12,16},{16,20},{20,24},{24,28},{28,32},{32,36}... | collective-permute-start | bytes 1966088 | tf_op jit(solution)/shard_map/ppermute | solution.py:63
  30.3 47.8 %collective-permute-start.10 = (bf16[160,2048]{1,0:T(8,128)(2,1)}, bf16[160,2048]{1,0:T(8,128)(2,1)}, u32[]{:S(2)}, u32[]{:S(2)}) collective-permute-start(bf16[160,2048]{1,0:T(8,128)(2,1)} %param.23), channel_id=1, source_target_pairs={{0,1},{1,0},{2,3},{3,2},{4,5},{5,4},{6,7},{7,6},{8,9},{9,8},{10,11... | collective-permute-start | bytes 1966088 | tf_op jit(solution)/shard_map/ppermute | solution.py:38
  37.4 39.8 %collective-permute-start.11 = (bf16[160,2048]{1,0:T(8,128)(2,1)}, bf16[160,2048]{1,0:T(8,128)(2,1)}, u32[]{:S(2)}, u32[]{:S(2)}) collective-permute-start(bf16[160,2048]{1,0:T(8,128)(2,1)} %param.23), channel_id=1, source_target_pairs={{0,2},{1,3},{2,0},{3,1},{4,6},{5,7},{6,4},{7,5},{8,10},{9,11},{10,... | collective-permute-start | bytes 1966088 | tf_op jit(solution)/shard_map/ppermute | solution.py:42
  41.8 66.2 %collective-permute-start.13 = (bf16[160,2048]{1,0:T(8,128)(2,1)}, bf16[160,2048]{1,0:T(8,128)(2,1)}, u32[]{:S(2)}, u32[]{:S(2)}) collective-permute-start(bf16[160,2048]{1,0:T(8,128)(2,1)} %param.24), channel_id=1, source_target_pairs={{0,1},{1,0},{2,3},{3,2},{4,5},{5,4},{6,7},{7,6},{8,9},{9,8},{10,11... | collective-permute-start | bytes 1966088 | tf_op jit(solution)/shard_map/ppermute | solution.py:38
  41.8 32.8 %collective-permute-start.9 = (bf16[256,640]{1,0:T(8,128)(2,1)}, bf16[256,640]{1,0:T(8,128)(2,1)}, u32[]{:S(2)}, u32[]{:S(2)}) collective-permute-start(bf16[256,640]{1,0:T(8,128)(2,1)} %collective-permute-done.8), channel_id=1, source_target_pairs={{0,1},{1,0},{2,3},{3,2},{4,5},{5,4},{6,7},{7,6},{8,9},{9,8},{10,11... | collective-permute-start | bytes 983048 | tf_op jit(solution)/shard_map/ppermute | solution.py:38
  69.7 20.6 %collective-permute-start.14 = (bf16[160,2048]{1,0:T(8,128)(2,1)}, bf16[160,2048]{1,0:T(8,128)(2,1)S(1)}, u32[]{:S(2)}, u32[]{:S(2)}) collective-permute-start(bf16[160,2048]{1,0:T(8,128)(2,1)} %param.24), channel_id=1, source_target_pairs={{0,66},{1,67},{2,64},{3,65},{4,70},{5,71},{6,68},{7,69},{8,74},{9,... | collective-permute-start | bytes 1966088 | tf_op jit(solution)/shard_map/ppermute | solution.py:46
  74.6 29.4 %collective-permute-start.17 = (bf16[512,640]{1,0:T(8,128)(2,1)S(1)}, bf16[512,640]{1,0:T(8,128)(2,1)S(1)}, u32[]{:S(2)}, u32[]{:S(2)}) collective-permute-start(bf16[512,640]{1,0:T(8,128)(2,1)S(1)} %copy-done.23), channel_id=1, source_target_pairs={{0,66},{1,67},{2,64},{3,65},{4,70},{5,71},{6,68},{7,69},{8,74},{9,... | collective-permute-start | bytes 1966088 | tf_op jit(solution)/shard_map/ppermute | solution.py:46
  77.2 27.2 %collective-permute-start.12 = (bf16[160,2048]{1,0:T(8,128)(2,1)}, bf16[160,2048]{1,0:T(8,128)(2,1)S(1)}, u32[]{:S(2)}, u32[]{:S(2)}) collective-permute-start(bf16[160,2048]{1,0:T(8,128)(2,1)} %collective-permute-done.11), channel_id=1, source_target_pairs={{0,1},{1,0},{2,3},{3,2},{4,5},{5,4},{6,7},{7,6},{8,9},{9,8},{10,11... | collective-permute-start | bytes 1966088 | tf_op jit(solution)/shard_map/ppermute | solution.py:38
  78.1 34.4 %collective-permute-start.16 = (bf16[512,640]{1,0:T(8,128)(2,1)S(1)}, bf16[512,640]{1,0:T(8,128)(2,1)S(1)}, u32[]{:S(2)}, u32[]{:S(2)}) collective-permute-start(bf16[512,640]{1,0:T(8,128)(2,1)S(1)} %copy-done.23), channel_id=1, source_target_pairs={{0,1},{1,0},{2,3},{3,2},{4,5},{5,4},{6,7},{7,6},{8,9},{9,8},{10,11... | collective-permute-start | bytes 1966088 | tf_op jit(solution)/shard_map/ppermute | solution.py:38
  90.3 17.6 %collective-permute-start.15 = (bf16[160,2048]{1,0:T(8,128)(2,1)S(1)}, bf16[160,2048]{1,0:T(8,128)(2,1)S(1)}, u32[]{:S(2)}, u32[]{:S(2)}) collective-permute-start(bf16[160,2048]{1,0:T(8,128)(2,1)S(1)} %collective-permute-done.14), channel_id=1, source_target_pairs={{0,1},{1,0},{2,3},{3,2},{4,5},{5,4},{6,7},{7,6},{8,9},{9,8},{10,11... | collective-permute-start | bytes 1966088 | tf_op jit(solution)/shard_map/ppermute | solution.py:38
  165.3 34.6 %collective-permute-start.19 = (bf16[512,640]{1,0:T(8,128)(2,1)}, bf16[512,640]{1,0:T(8,128)(2,1)}, u32[]{:S(2)}, u32[]{:S(2)}) collective-permute-start(bf16[512,640]{1,0:T(8,128)(2,1)} %slice.280), channel_id=1, source_target_pairs={{4,0},{8,4},{12,8},{16,12},{20,16},{24,20},{28,24},{32,28},{36,32}... | collective-permute-start | bytes 1966088 | tf_op jit(solution)/shard_map/ppermute | solution.py:63
  219.9 10.8 %collective-permute-start.22 = (bf16[2,4,104,128]{3,2,0,1:T(8,128)(2,1)S(1)}, bf16[2,4,104,128]{3,2,0,1:T(8,128)(2,1)S(1)}, u32[]{:S(2)}, u32[]{:S(2)}) collective-permute-start(bf16[2,4,104,128]{3,2,0,1:T(8,128)(2,1)S(1)} %bitcast.431), channel_id=1, source_target_pairs={{0,48},{4,52},{8,56},{12,60},{16,0},{20,4},{24,8},{28,12},{32,16},... | collective-permute-start | bytes 638984 | tf_op jit(solution)/shard_map/ppermute | solution.py:54
  222.3 60.5 %collective-permute-start.48 = (bf16[2,7680,128]{2,1,0:T(8,128)(2,1)S(1)}, bf16[2,7680,128]{2,1,0:T(8,128)(2,1)S(1)}, u32[]{:S(2)}, u32[]{:S(2)}) collective-permute-start(bf16[2,7680,128]{2,1,0:T(8,128)(2,1)S(1)} %dynamic-slice_bitcast_fusion), channel_id=1, source_target_pairs={{0,1},{1,0},{2,3},{3,2},{4,5},{5,4},{6,7},{7,6},{8,9},{9,8},{10,11... | collective-permute-start | bytes 11796488 | tf_op jit(solution)/shard_map/ppermute | solution.py:38
  232.9 11.9 %collective-permute-start.25 = (bf16[2,104,128]{2,1,0:T(8,128)(2,1)S(1)}, bf16[2,104,128]{2,1,0:T(8,128)(2,1)S(1)}, u32[]{:S(2)}, u32[]{:S(2)}) collective-permute-start(bf16[2,104,128]{2,1,0:T(8,128)(2,1)S(1)} %get-tuple-element.209), channel_id=1, source_target_pairs={{0,12},{4,0},{8,4},{12,8},{16,28},{20,16},{24,20},{28,24},{32,44},... | collective-permute-start | bytes 159752 | tf_op jit(solution)/shard_map/ppermute | solution.py:58
  284.4 13.5 %collective-permute-start.51 = (bf16[2,4,240,128]{3,2,0,1:T(8,128)(2,1)S(1)}, bf16[2,4,240,128]{3,2,0,1:T(8,128)(2,1)S(1)}, u32[]{:S(2)}, u32[]{:S(2)}) collective-permute-start(bf16[2,4,240,128]{3,2,0,1:T(8,128)(2,1)S(1)} %bitcast.423), channel_id=1, source_target_pairs={{0,32},{4,36},{8,40},{12,44},{16,48},{20,52},{24,56},{28,60},{32,0... | collective-permute-start | bytes 1474568 | tf_op jit(solution)/shard_map/ppermute | solution.py:54
  291.2 14.5 %collective-permute-start.49 = (bf16[2,4,240,128]{3,2,0,1:T(8,128)(2,1)S(1)}, bf16[2,4,240,128]{3,2,0,1:T(8,128)(2,1)S(1)}, u32[]{:S(2)}, u32[]{:S(2)}) collective-permute-start(bf16[2,4,240,128]{3,2,0,1:T(8,128)(2,1)S(1)} %bitcast.422), channel_id=1, source_target_pairs={{0,16},{4,20},{8,24},{12,28},{16,32},{20,36},{24,40},{28,44},{32,4... | collective-permute-start | bytes 1474568 | tf_op jit(solution)/shard_map/ppermute | solution.py:54
  294.1 17.1 %collective-permute-start.57 = (bf16[2,4,240,128]{3,2,1,0:T(8,128)(2,1)S(1)}, bf16[2,4,240,128]{3,2,1,0:T(8,128)(2,1)S(1)}, u32[]{:S(2)}, u32[]{:S(2)}) collective-permute-start(bf16[2,4,240,128]{3,2,1,0:T(8,128)(2,1)S(1)} %get-tuple-element.129), channel_id=1, source_target_pairs={{0,8},{4,12},{8,0},{12,4},{16,24},{20,28},{24,16},{28,20},{32,40},... | collective-permute-start | bytes 1474568 | tf_op jit(solution)/shard_map/ppermute | solution.py:58
  296.8 16.4 %collective-permute-start.56 = (bf16[2,4,240,128]{3,2,1,0:T(8,128)(2,1)S(1)}, bf16[2,4,240,128]{3,2,1,0:T(8,128)(2,1)S(1)}, u32[]{:S(2)}, u32[]{:S(2)}) collective-permute-start(bf16[2,4,240,128]{3,2,1,0:T(8,128)(2,1)S(1)} %get-tuple-element.130), channel_id=1, source_target_pairs={{0,12},{4,0},{8,4},{12,8},{16,28},{20,16},{24,20},{28,24},{32,44},... | collective-permute-start | bytes 1474568 | tf_op jit(solution)/shard_map/ppermute | solution.py:58
  297.9 15.3 %collective-permute-start.55 = (bf16[2,4,240,128]{3,2,1,0:T(8,128)(2,1)S(1)}, bf16[2,4,240,128]{3,2,1,0:T(8,128)(2,1)S(1)}, u32[]{:S(2)}, u32[]{:S(2)}) collective-permute-start(bf16[2,4,240,128]{3,2,1,0:T(8,128)(2,1)S(1)} %get-tuple-element.128), channel_id=1, source_target_pairs={{0,4},{4,8},{8,12},{12,0},{16,20},{20,24},{24,28},{28,16},{32,36},... | collective-permute-start | bytes 1474568 | tf_op jit(solution)/shard_map/ppermute | solution.py:58
  (132 other events, 825.9 us)
